TPU v7x, 32 devices: a whole 2x2x4 slice. The times are simulated.
32 devices in a mesh: req: 4 (over y, x), tile: 4 (over z), col: 2 (over core).
Axes of the slice: x: 2, y: 2, z: 4, core: 2. Of those that a mesh axis runs over, the one named last changes fastest.
Arguments:
- img_qkv: bfloat16 [4, 64, 64, 3, 1536], P('req', 'tile', None, None, 'col'), may hold values from -10 to 10
- txt_kv: bfloat16 [4, 512, 2, 1536], P('req', 'tile', None, 'col'), may hold values from -8 to 8
- text_len: int32 [4], P('req'), may hold values from 256 to 512, as said below
- hidden_state: bfloat16 [4, 64, 64, 3072], P('req', 'tile', 'col'), may hold values from -3 to 3
- modulation: float32 [28, 4, 3, 3072], P(None, 'req'), may hold values from 0.1 to 1.9
- w_attn_out: bfloat16 [1536, 3072], replicated, may hold values from -0.15625 to 0.15625
- w_final: bfloat16 [3072, 64], replicated, may hold values from -0.109375 to 0.109375
- latent: float32 [4, 64, 64, 64], P('req', 'tile', 'col'), may hold values from -6 to 6
- sigmas: float32 [29], replicated, may hold values from -1 to 3, as said below
- step_index: int32 [1], replicated, may hold values from 0 to 27
- w_preview: float32 [3, 3, 64, 64], replicated, may hold values from -0.25 to 0.25
Outputs:
- velocity: float32 [4, 64, 64, 64], P('req', 'tile', 'col')
- latent_next: float32 [4, 64, 64, 64], P('req', 'tile', 'col')
- preview: float32 [4, 64, 64, 64], P('req', 'tile', 'col')
Inputs may be any that keep to these rules, and one draw needn't show every extreme that they name: `text_len`: some request has exactly 512 live text tokens. sigmas[i] - sigmas[i + 1] lies between 0.1 / 28 and 3.4 / 28.
All inputs are finite; a program needn't handle non-finite values.
Results may differ from a plain program's by a relative error of at most 0.005.
Values may be sent and summed in bfloat16 or wider, within the bound.
A program may use at most 320 MiB of HBM per device.

v0:
```python
import math
import jax
import jax.numpy as jnp
from jax import lax
from jax.sharding import PartitionSpec as P

HD = 128
norm_eps = 1e-06


def padded_2(cells, sides, width):
    for axis, dim in sides:
        count = lax.axis_size(axis)
        ends = count - 1
        head = lax.slice_in_dim(cells, 0, width, axis=dim)
        tail = lax.slice_in_dim(cells, cells.shape[dim] - width, cells.shape[dim], axis=dim)
        cells = jnp.concatenate(
            [
                lax.ppermute(tail, axis, [(i, (i + 1) % count) for i in range(ends)]),
                cells,
                lax.ppermute(head, axis, [((i + 1) % count, i) for i in range(ends)]),
            ],
            axis=dim,
        )
    return cells


def make_fold(queries, img_rows, text_rows, text_limit):
    score_scale = 1.0 / math.sqrt(HD)
    shard_rows = img_rows + text_rows

    def fold_step(carry, piece, start):
        run_max, run_sum, run_acc = carry
        piece_len = piece.shape[0]
        key_index = jnp.arange(piece_len, dtype=jnp.int32)
        in_shard = key_index % shard_rows
        text_pos = key_index // shard_rows * text_rows + in_shard - img_rows
        key_live = (in_shard < img_rows) | (text_pos < text_limit)
        scores = (
            jnp.einsum("qhd,khd->hqk", queries, piece[:, 0], preferred_element_type=jnp.float32)
            * score_scale
        )
        scores = jnp.where(key_live[None, None, :], scores, -1e30)
        new_max = jnp.maximum(run_max, jnp.max(scores, axis=2))
        weights = jnp.where(key_live[None, None, :], jnp.exp(scores - new_max[:, :, None]), 0.0)
        run_sum = jnp.sum(weights, axis=2)
        run_acc = jnp.einsum(
            "hqk,khd->hqd",
            weights.astype(jnp.bfloat16),
            piece[:, 1],
            preferred_element_type=jnp.float32,
        )
        return (new_max, run_sum, run_acc)

    return fold_step


def start_carry(query_rows, head_count):
    return (
        jnp.full((head_count, query_rows), -1e30, jnp.float32),
        jnp.zeros((head_count, query_rows), jnp.float32),
        jnp.zeros((head_count, query_rows, HD), jnp.float32),
    )


def finish(carry):
    run_max, run_sum, run_acc = carry
    return jnp.transpose(run_acc / run_sum[:, :, None], (1, 0, 2)).astype(jnp.bfloat16)


def body(
    img_qkv,
    txt_kv,
    text_len,
    hidden_state,
    modulation,
    w_attn_out,
    w_final,
    latent,
    sigmas,
    step_index,
    w_preview,
):
    tile_rows = img_qkv.shape[1]
    grid_cols = img_qkv.shape[2]
    local_heads = img_qkv.shape[4] // HD
    text_rows = txt_kv.shape[1]
    tile_cols = hidden_state.shape[2]
    col_count = grid_cols // tile_cols
    own_rows = tile_rows * tile_cols
    text_limit = text_len[0]
    all_heads = local_heads * col_count
    img_block = img_qkv[0].reshape(tile_rows, grid_cols, 3, local_heads, HD)
    txt_block = txt_kv[0].reshape(1, text_rows, 2, local_heads, HD)
    img_mixed, txt_mixed = (
        lax.all_to_all(img_block, "col", split_axis=1, concat_axis=3, tiled=True),
        lax.all_to_all(txt_block, "col", split_axis=1, concat_axis=3, tiled=True),
    )
    img_flat = img_mixed.reshape(own_rows, 3, all_heads, HD)
    txt_flat = txt_mixed.reshape(text_rows // col_count, 2, all_heads, HD)
    key_value = jnp.concatenate([img_flat[:, 1:], txt_flat], axis=0)
    fold_step = make_fold(img_flat[:, 0], own_rows, text_rows // col_count, text_limit)
    carry = fold_step(
        start_carry(own_rows, all_heads),
        lax.all_gather(key_value, ("tile", "col"), axis=0, tiled=True),
        jnp.int32(0),
    )
    attended = finish(carry).reshape(own_rows, all_heads * HD)
    branch = jnp.dot(attended, w_attn_out, preferred_element_type=jnp.float32)
    step_now = step_index[0]
    mod_now = lax.dynamic_index_in_dim(modulation, step_now, 0, keepdims=False)[0]
    width = hidden_state.shape[3]
    mixed_state = (
        hidden_state[0].reshape(own_rows, width).astype(jnp.float32) + mod_now[0][None, :] * branch
    )
    row_mean = jnp.mean(mixed_state, axis=1, keepdims=True)
    centred = mixed_state - row_mean
    row_var = jnp.mean(centred * centred, axis=1, keepdims=True)
    normed = (
        centred / jnp.sqrt(row_var + norm_eps) * (1.0 + mod_now[2][None, :]) + mod_now[1][None, :]
    )
    normed = normed.astype(jnp.bfloat16)
    velocity = jnp.dot(normed, w_final, preferred_element_type=jnp.float32)
    channels = velocity.shape[1]
    sigma_step = sigmas[step_now + 1] - sigmas[step_now]
    updated = latent[0].reshape(own_rows, channels) + sigma_step * velocity
    grid_field = updated.reshape(tile_rows, tile_cols, channels)
    padded = padded_2(grid_field, (("tile", 0), ("col", 1)), 1)
    preview = jnp.zeros((tile_rows, tile_cols, channels), jnp.float32)
    for row_off in range(3):
        for col_off in range(3):
            preview = preview + jnp.einsum(
                "yxc,cd->yxd",
                padded[row_off : row_off + tile_rows, col_off : col_off + tile_cols],
                w_preview[row_off, col_off],
                precision=lax.Precision.HIGHEST,
            )
    return (velocity.reshape(1, tile_rows, tile_cols, channels), grid_field[None], preview[None])


def solution(mesh):
    placed = (
        P("req", "tile", None, None, "col"),
        P("req", "tile", None, "col"),
        P("req"),
        P("req", "tile", "col", None),
        P(None, "req", None, None),
        P(),
        P(),
        P("req", "tile", "col", None),
        P(),
        P(),
        P(),
    )
    return jax.shard_map(
        body,
        mesh=mesh,
        in_specs=placed,
        out_specs=(
            P("req", "tile", "col", None),
            P("req", "tile", "col", None),
            P("req", "tile", "col", None),
        ),
        check_vma=False,
    )
```

profile of v0, /device:TPU:0, one launch (start us, length us, event | category | flops | bytes accessed | tf_op | source)
XLA Modules:
  0.0 456.4 jit_solution(9621636207864728363)
XLA Ops:
  7.2 0.0 copy-start
  7.2 10.8 %reshape_squeeze.10 = bf16[16,64,3,6,128]{4,3,1,2,0:T(8,128)(2,1)} reshape(bf16[1,16,64,3,768]{4,2,3,1,0:T(8,128)(2,1)} %param.11) | data formatting | bytes 9437184 | tf_op jit(solution)/shard_map/reshape;squeeze | solution.py:93
  18.0 10.5 %copy.59 = bf16[16,64,3,6,128]{4,0,3,2,1:T(8,128)(2,1)} copy(bf16[16,64,3,6,128]{4,3,1,2,0:T(8,128)(2,1)} %reshape_squeeze.10) | data formatting | bytes 9437184 | tf_op jit(solution)/shard_map/reshape;squeeze | solution.py:93
  28.5 0.0 copy-start.3
  28.5 5.9 %all-to-all-start = ((bf16[16,64,3,6,128]{4,0,3,2,1:T(8,128)(2,1)}), bf16[16,64,3,6,128]{4,0,3,2,1:T(8,128)(2,1)}, u32[]{:S(2)}, u32[]{:S(2)}) async-start(bf16[16,64,3,6,128]{4,0,3,2,1:T(8,128)(2,1)} %copy.59), calls=%async_computation | async-start | bytes 9437184 | tf_op jit(solution)/shard_map/all_to_all | solution.py:96
  34.4 0.0 copy-done.3
  34.4 0.5 copy.62
  34.9 1.1 copy.63
  36.0 3.3 all-to-all-done
  39.2 4.2 all-to-all-start.1
  43.4 0.0 all-gather.2.cloned.1.call-start
  43.5 4.2 copy.61
  47.6 0.0 copy-start.1
  47.6 2.1 copy-done.1
  49.8 0.3 slice.131
  50.1 0.0 copy-start.5
  50.1 0.0 all-to-all-done.1
  50.1 1.1 copy.64
  51.2 2.0 pad_maximum_fusion
  53.2 0.0 all-gather.2.cloned.1.call-update
  54.6 1.1 copy.69
  55.7 0.0 copy-done.5
  55.7 0.6 fusion.73
  57.6 0.8 dynamic-slice_add_fusion
  58.4 243.5 %all-gather.2.cloned.1.call-done = bf16[4608,2,12,128]{3,0,2,1:T(8,128)(2,1)} async-done(((bf16[576,2,12,128]{3,0,2,1:T(8,128)(2,1)}), bf16[4608,2,12,128]{3,0,2,1:T(8,128)(2,1)}) %all-gather.2.cloned.1.call-update) | async-done | bytes 28311568 | tf_op jit(solution)/shard_map/all_gather | solution.py:105
  301.9 43.7 %bitcast_reduce_fusion = (f32[12,512]{1,0:T(8,128)S(1)}, f32[12,4608,512]{2,1,0:T(8,128)}) fusion(pred[4608]{0:T(1024)(128)(4,1)S(1)} %fusion.67, bf16[512,3,12,128]{3,0,2,1:T(8,128)(2,1)} %bitcast.136, bf16[4608,2,12,128]{3,0,2,1:T(8,128)(2,1)} %all-gather.2.cloned.1.call-done), kind=kOutput, calls=%fused_computation.1 | convolution fusion | flops 7332685824 | bytes 129004032 | tf_op jit(solution)/shard_map/qhd,khd->hqk/dot_general | solution.py:40
  345.6 35.4 %fusion.2 = f32[12,512]{1,0:T(8,128)S(1)} fusion(f32[12,4608,512]{2,1,0:T(8,128)} %get-tuple-element.18, f32[12,512]{1,0:T(8,128)S(1)} %broadcast_maximum_fusion, pred[4608]{0:T(1024)(128)(4,1)S(1)} %fusion.67), kind=kLoop, calls=%fused_computation.5 | loop fusion | flops 141551616 | bytes 113299968 | tf_op jit(solution)/shard_map/reduce_sum | solution.py:46
  381.0 42.5 %fusion.9 = bf16[512,12,128]{0,2,1:T(8,128)(2,1)S(1)} fusion(bf16[4608,2,12,128]{3,0,2,1:T(8,128)(2,1)} %all-gather.2.cloned.1.call-done, f32[12,4608,512]{2,1,0:T(8,128)} %get-tuple-element.18, f32[12,512]{1,0:T(8,128)S(1)} %broadcast_maximum_fusion, pred[4608]{0:T(1024)(128)(4,1)S(1)} %fusion.67, f32[512,12]{0,1:T(8,128)S(1)} %bitcast.148), kind=kOutput, calls=%fused_computation.18 | convolution fusion | flops 7390887936 | bytes 129050624 | tf_op jit(solution)/shard_map/hqk,khd->hqd/dot_general | solution.py:47
  423.5 9.1 %fusion.74 = (f32[512]{0:T(512)S(1)}, f32[512,3072]{1,0:T(8,128)S(1)}) fusion(bf16[512,1536]{0,1:T(8,128)(2,1)S(1)} %bitcast.153, bf16[1536,3072]{1,0:T(8,128)(2,1)} %param.16, f32[3072]{0:T(1024)S(1)} %bitcast.151, bf16[512,3072]{1,0:T(8,128)(2,1)} %bitcast.152), kind=kOutput, calls=%fused_computation.103 | convolution fusion | flops 4838129152 | bytes 20461568 | tf_op jit(solution)/shard_map/dot_general | solution.py:109
  432.6 0.8 multiply_reduce_fusion
  433.3 0.0 copy-done
  433.3 0.0 copy-start.4
  433.3 1.4 multiply_add_fusion
  434.8 0.1 copy.70
  434.9 0.0 copy-start.2
  434.9 0.1 slice_bitcast_fusion.9
  435.0 1.3 collective-permute-start
  436.3 1.3 collective-permute-start.1
  437.6 0.0 copy-done.4
  437.6 0.4 fusion.42
  438.0 0.8 copy.68
  438.8 0.0 collective-permute-done
  438.8 0.1 copy.72
  438.9 0.4 fusion.20
  439.2 2.9 collective-permute-done.1
  442.1 0.1 copy.73
  442.2 1.3 collective-permute-start.2
  443.5 1.3 collective-permute-start.3
  444.8 0.4 fusion.24
  445.2 0.0 collective-permute-done.2
  445.2 1.4 collective-permute-done.3
  446.6 0.1 maximum_maximum_fusion
  446.6 0.3 fusion.35
  447.0 0.4 fusion.28
  447.3 0.4 fusion.33
  447.7 0.4 fusion.30
  448.1 0.4 fusion.17
  448.5 1.1 fusion.19
  449.5 0.0 copy-done.2
  (6 shorter events, 0.1 us)
Async XLA Ops:
  7.2 426.2 %copy-start = (bf16[3072,64]{0,1:T(8,128)(2,1)S(1)}, bf16[3072,64]{0,1:T(8,128)(2,1)}, u32[]{:S(2)}) copy-start(bf16[3072,64]{0,1:T(8,128)(2,1)} %param.17) | copy-start | bytes 1179652
  28.5 5.9 %copy-start.3 = (bf16[1,128,2,768]{3,2,1,0:T(2,128)(2,1)S(1)}, bf16[1,128,2,768]{3,2,1,0:T(2,128)(2,1)}, u32[]{:S(2)}) copy-start(bf16[1,128,2,768]{3,2,1,0:T(2,128)(2,1)} %param.12) | copy-start | bytes 1179652
  28.5 10.8 %all-to-all-start = ((bf16[16,64,3,6,128]{4,0,3,2,1:T(8,128)(2,1)}), bf16[16,64,3,6,128]{4,0,3,2,1:T(8,128)(2,1)}, u32[]{:S(2)}, u32[]{:S(2)}) async-start(bf16[16,64,3,6,128]{4,0,3,2,1:T(8,128)(2,1)} %copy.59), calls=%async_computation | async-start | bytes 9437184 | tf_op jit(solution)/shard_map/all_to_all | solution.py:96
  39.2 10.8 %all-to-all-start.1 = ((bf16[1,128,2,6,128]{4,2,3,0,1:T(2,128)(2,1)}), bf16[1,128,2,6,128]{4,2,3,0,1:T(2,128)(2,1)}, u32[]{:S(2)}, u32[]{:S(2)}) async-start(bf16[1,128,2,6,128]{4,2,3,0,1:T(2,128)(2,1)} %copy.63), calls=%async_computation.1 | async-start | bytes 786432 | tf_op jit(solution)/shard_map/all_to_all | solution.py:97
  43.4 258.5 %all-gather.2.cloned.1.call-start = ((), (), s32[]{:S(2)}) async-start(), calls=%async_computation.2 | async-start | bytes 31850496 | tf_op jit(solution)/shard_map/all_gather | solution.py:105
  47.6 2.1 copy-start.1
  50.1 5.6 %copy-start.5 = (f32[29]{0:T(128)S(1)}, f32[29]{0:T(128)}, u32[]{:S(2)}) copy-start(f32[29]{0:T(128)} %param.19) | copy-start | bytes 352
  433.3 4.3 copy-start.4
  434.9 14.6 %copy-start.2 = (f32[512,64]{1,0:T(8,128)}, f32[512,64]{1,0:T(8,128)S(1)}, u32[]{:S(2)}) copy-start(f32[512,64]{1,0:T(8,128)S(1)} %copy.70) | copy-start | bytes 393220
  435.0 3.8 collective-permute-start
  436.3 5.8 %collective-permute-start.1 = (f32[1,32,64]{1,2,0:T(8,128)S(1)}, f32[1,32,64]{1,2,0:T(8,128)S(1)}, u32[]{:S(2)}, u32[]{:S(2)}) collective-permute-start(f32[1,32,64]{1,2,0:T(8,128)S(1)} %get-tuple-element.14), channel_id=1, source_target_pairs={{2,0},{4,2},{6,4},{3,1},{5,3},{7,5},{10,8},{12,10},{14,12},{11,9},... | collective-permute-start | bytes 24584 | tf_op jit(solution)/shard_map/ppermute | solution.py:21
  442.2 3.0 collective-permute-start.2
  443.5 3.1 collective-permute-start.3
Sparse Core Ops, SparseCore 0:
  53.4 248.4 all-gather.1
where the time goes:
time: 457 us; the launch traced here: 456 us
  waiting for transfers between devices  251 us (55%)
  matrix products  101 us (22%)
  other arithmetic  39.1 us (9%)
  local copies, waits for them, and re-layouts  33.4 us (7%)
  between operations  17 us (4%)
  starting transfers between devices  15.3 us (3%)
    all_gather x1, waiting for transfers between devices, body(): lax.all_gather(key_value, ('tile', 'col'), axis=0, tiled=True)  244 us
    dot_general x1, matrix products, fold_step(): jnp.einsum('qhd,khd->hqk', queries, piece[:, 0], preferred_element_type=j...  43.7 us
    dot_general x1, matrix products, fold_step(): jnp.einsum('hqk,khd->hqd', weights.astype(jnp.bfloat16), piece[:, 1], pre...  42.5 us
    reduce_sum x1, other arithmetic, fold_step(): run_sum = jnp.sum(weights, axis=2)  35.4 us
    another operation x2, local copies, waits for them, and re-layouts, body(): img_block = img_qkv[0].reshape(tile_rows, grid_cols, 3, local_heads, HD)  21.3 us
  transfers between devices with their start and end apart: 7, of which 4 were waited for; matrix products, arithmetic and copies ran while one was open for 2% of the time, Pallas kernels for 0%

commit v1 on v0

--- a/solution.py
+++ b/solution.py
@@ -6,6 +6,37 @@
 
 HD = 128
 norm_eps = 1e-06
+
+
+def note_the_slices(obj, a_name):
+    extra = jax.lax.axis_size(a_name)
+    fresh = jax.lax.axis_index(a_name)
+    later, part_now, out_arr = (extra, fresh, obj.shape[0])
+    outcome_arr = lax.dynamic_update_slice_in_dim(
+        jnp.zeros([rr * later if dev == 0 else rr for dev, rr in enumerate(obj.shape)], obj.dtype),
+        obj,
+        part_now * out_arr,
+        axis=0,
+    )
+    t_next = a_now = obj
+    for it in range(1, later // 2 + 1):
+        t_next = jax.lax.ppermute(
+            t_next,
+            axis_name=a_name,
+            perm=list(map(lambda dev: (dev, (dev + 1) % later), range(later))),
+        )
+        outcome_arr = lax.dynamic_update_slice_in_dim(
+            outcome_arr, t_next, (part_now - it) % later * out_arr, axis=0
+        )
+        if 2 * it < later:
+            y_new = range(later)
+            local_out = map(lambda dev: (dev, (dev - 1) % later), y_new)
+            clean = list(local_out)
+            a_now = jax.lax.ppermute(a_now, axis_name=a_name, perm=clean)
+            outcome_arr = lax.dynamic_update_slice_in_dim(
+                outcome_arr, a_now, (part_now + it) % later * out_arr, axis=0
+            )
+    return outcome_arr
 
 
 def padded_2(cells, sides, width):
@@ -101,9 +132,7 @@
     key_value = jnp.concatenate([img_flat[:, 1:], txt_flat], axis=0)
     fold_step = make_fold(img_flat[:, 0], own_rows, text_rows // col_count, text_limit)
     carry = fold_step(
-        start_carry(own_rows, all_heads),
-        lax.all_gather(key_value, ("tile", "col"), axis=0, tiled=True),
-        jnp.int32(0),
+        start_carry(own_rows, all_heads), note_the_slices(key_value, ("tile", "col")), jnp.int32(0)
     )
     attended = finish(carry).reshape(own_rows, all_heads * HD)
     branch = jnp.dot(attended, w_attn_out, preferred_element_type=jnp.float32)

time: 457 us -> 494 us (1.081)
  local copies, waits for them, and re-layouts: 33.4 us -> 74.9 us
  between operations: 17 us -> 4.47 us
  starting transfers between devices: 15.3 us -> 27.3 us
  waiting for transfers between devices: 251 us -> 246 us
    all_gather x1 -> x0, waiting for transfers between devices: 244 us -> none  [body(): lax.all_gather(key_value, ('tile', 'col'), axis=0, tiled=True)]
    ppermute x0 -> x7, waiting for transfers between devices: none -> 237 us  [the longest x4 237 us: note_the_slices(): jax.lax.ppermute(t_next, axis_name=a_name, perm=list(map(lambda dev: (dev...]
    dynamic_update_slice x0 -> x7, local copies, waits for them, and re-layouts: none -> 27 us  [the longest x4 15.7 us: note_the_slices(): lax.dynamic_update_slice_in_dim(outcome_arr, t_next, (part_now - it) % la...]
    ppermute x0 -> x7, starting transfers between devices: none -> 10.4 us  [the longest x3 9.97 us: note_the_slices(): a_now = jax.lax.ppermute(a_now, axis_name=a_name, perm=clean)]
    broadcast_in_dim x0 -> x1, local copies, waits for them, and re-layouts: none -> 9.49 us  [note_the_slices(): jnp.zeros([rr * later if dev == 0 else rr for dev, rr in enumerate(obj.sh...]
  transfers between devices with their start and end apart: 7 -> 13, of which waited for: 4 -> 7; matrix products, arithmetic and copies ran while one was open for 2% -> 7% of each run, Pallas kernels for 0% -> 0%
where the time goes in v1:
time: 494 us
  waiting for transfers between devices  246 us (50%)
  matrix products  101 us (20%)
  local copies, waits for them, and re-layouts  74.9 us (15%)
  other arithmetic  40.5 us (8%)
  starting transfers between devices  27.3 us (6%)
    ppermute x4, waiting for transfers between devices, note_the_slices(): jax.lax.ppermute(t_next, axis_name=a_name, perm=list(map(lambda dev: (dev...  237 us
    dot_general x1, matrix products, fold_step(): jnp.einsum('qhd,khd->hqk', queries, piece[:, 0], preferred_element_type=j...  43.7 us
    dot_general x1, matrix products, fold_step(): jnp.einsum('hqk,khd->hqd', weights.astype(jnp.bfloat16), piece[:, 1], pre...  42.6 us
    reduce_sum x1, other arithmetic, fold_step(): run_sum = jnp.sum(weights, axis=2)  35.4 us
    another operation x2, local copies, waits for them, and re-layouts, body(): img_block = img_qkv[0].reshape(tile_rows, grid_cols, 3, local_heads, HD)  21.4 us
    dynamic_update_slice x4, local copies, waits for them, and re-layouts, note_the_slices(): lax.dynamic_update_slice_in_dim(outcome_arr, t_next, (part_now - it) % la...  15.7 us
    dynamic_update_slice x3, local copies, waits for them, and re-layouts, note_the_slices(): lax.dynamic_update_slice_in_dim(outcome_arr, a_now, (part_now + it) % lat...  11.3 us
    ppermute x3, starting transfers between devices, note_the_slices(): a_now = jax.lax.ppermute(a_now, axis_name=a_name, perm=clean)  9.97 us
  transfers between devices with their start and end apart: 13, of which 7 were waited for; matrix products, arithmetic and copies ran while one was open for 7% of the time, Pallas kernels for 0%

profile of v1, /device:TPU:0, one launch (start us, length us, event | category | flops | bytes accessed | tf_op | source)
XLA Modules:
  0.0 493.5 jit_solution(17110702152974670532)
XLA Ops:
  0.6 0.0 copy-start
  0.6 10.8 %reshape_squeeze.10 = bf16[16,64,3,6,128]{4,3,1,2,0:T(8,128)(2,1)} reshape(bf16[1,16,64,3,768]{4,2,3,1,0:T(8,128)(2,1)} %param.11) | data formatting | bytes 9437184 | tf_op jit(solution)/shard_map/reshape;squeeze | solution.py:124
  11.5 10.5 %copy.59 = bf16[16,64,3,6,128]{4,0,3,2,1:T(8,128)(2,1)} copy(bf16[16,64,3,6,128]{4,3,1,2,0:T(8,128)(2,1)} %reshape_squeeze.10) | data formatting | bytes 9437184 | tf_op jit(solution)/shard_map/reshape;squeeze | solution.py:124
  22.0 5.8 %all-to-all-start = ((bf16[16,64,3,6,128]{4,0,3,2,1:T(8,128)(2,1)}), bf16[16,64,3,6,128]{4,0,3,2,1:T(8,128)(2,1)}, u32[]{:S(2)}, u32[]{:S(2)}) async-start(bf16[16,64,3,6,128]{4,0,3,2,1:T(8,128)(2,1)} %copy.59), calls=%async_computation | async-start | bytes 9437184 | tf_op jit(solution)/shard_map/all_to_all | solution.py:127
  27.8 0.5 copy.62
  28.3 1.1 copy.63
  29.4 3.3 all-to-all-done
  32.7 4.2 all-to-all-start.1
  36.8 4.2 copy.61
  41.0 2.1 copy-done.1
  43.2 0.3 slice.131
  43.5 1.1 copy.64
  44.5 0.8 copy.65
  45.3 9.5 %broadcast_in_dim.37 = bf16[4608,2,12,128]{3,0,2,1:T(8,128)(2,1)} broadcast(bf16[]{:T(256)} %constant.94.clone.1), dimensions={} | broadcast | bytes 28311554 | tf_op jit(solution)/shard_map/broadcast_in_dim | solution.py:16
  54.8 2.9 pad_maximum_fusion
  57.7 0.5 collective-permute-start
  58.2 4.6 collective-permute-start.1
  62.8 75.0 %collective-permute-done = bf16[576,2,12,128]{3,0,2,1:T(8,128)(2,1)S(1)} collective-permute-done((bf16[576,2,12,128]{3,0,2,1:T(8,128)(2,1)S(1)}, bf16[576,2,12,128]{3,0,2,1:T(8,128)(2,1)S(1)}, u32[]{:S(2)}, u32[]{:S(2)}) %collective-permute-start) | collective-permute-done | bytes 3538976 | tf_op jit(solution)/shard_map/ppermute | solution.py:23
  137.9 1.8 copy-done.3
  139.6 3.5 collective-permute-start.3
  143.2 74.8 %collective-permute-done.2 = bf16[576,2,12,128]{3,0,2,1:T(8,128)(2,1)S(1)} collective-permute-done((bf16[576,2,12,128]{3,0,2,1:T(8,128)(2,1)S(1)}, bf16[576,2,12,128]{3,0,2,1:T(8,128)(2,1)S(1)}, u32[]{:S(2)}, u32[]{:S(2)}) %collective-permute-start.2) | collective-permute-done | bytes 3538976 | tf_op jit(solution)/shard_map/ppermute | solution.py:23
  218.0 1.7 copy-done.6
  219.7 1.8 collective-permute-start.5
  221.5 74.1 %collective-permute-done.4 = bf16[576,2,12,128]{3,0,2,1:T(8,128)(2,1)} collective-permute-done((bf16[576,2,12,128]{3,0,2,1:T(8,128)(2,1)S(1)}, bf16[576,2,12,128]{3,0,2,1:T(8,128)(2,1)}, u32[]{:S(2)}, u32[]{:S(2)}) %collective-permute-start.4) | collective-permute-done | bytes 3538976 | tf_op jit(solution)/shard_map/ppermute | solution.py:23
  297.0 1.7 copy.69
  298.7 0.6 fusion.73
  301.5 1.4 dynamic-slice_add_fusion
  302.8 4.4 constant_dynamic-update-slice_fusion.6
  307.2 2.4 constant_dynamic-update-slice_fusion.5
  309.6 2.4 constant_dynamic-update-slice_fusion.4
  312.0 4.5 constant_dynamic-update-slice_fusion.3
  316.5 4.4 constant_dynamic-update-slice_fusion.2
  320.9 4.4 constant_dynamic-update-slice_fusion.1
  325.4 13.3 %collective-permute-done.6 = bf16[576,2,12,128]{3,0,2,1:T(8,128)(2,1)} collective-permute-done((bf16[576,2,12,128]{3,0,2,1:T(8,128)(2,1)}, bf16[576,2,12,128]{3,0,2,1:T(8,128)(2,1)}, u32[]{:S(2)}, u32[]{:S(2)}) %collective-permute-start.6) | collective-permute-done | bytes 3538976 | tf_op jit(solution)/shard_map/ppermute | solution.py:23
  338.7 4.4 constant_dynamic-update-slice_fusion
  343.1 43.7 %bitcast_reduce_fusion = (f32[12,512]{1,0:T(8,128)S(1)}, f32[12,4608,512]{2,1,0:T(8,128)}) fusion(pred[4608]{0:T(1024)(128)(4,1)S(1)} %fusion.65, bf16[512,3,12,128]{3,0,2,1:T(8,128)(2,1)} %bitcast.136, bf16[4608,2,12,128]{3,0,2,1:T(8,128)(2,1)} %constant_dynamic-update-slice_fusion), kind=kOutput, calls=%fused_computation.1 | convolution fusion | flops 7332685824 | bytes 129004032 | tf_op jit(solution)/shard_map/qhd,khd->hqk/dot_general | solution.py:71
  386.8 35.4 %fusion.2 = f32[12,512]{1,0:T(8,128)S(1)} fusion(f32[12,4608,512]{2,1,0:T(8,128)} %get-tuple-element.20, f32[12,512]{1,0:T(8,128)S(1)} %broadcast_maximum_fusion, pred[4608]{0:T(1024)(128)(4,1)S(1)} %fusion.65), kind=kLoop, calls=%fused_computation.5 | loop fusion | flops 141551616 | bytes 113299968 | tf_op jit(solution)/shard_map/reduce_sum | solution.py:77
  422.2 42.6 %fusion.9 = bf16[512,12,128]{0,2,1:T(8,128)(2,1)S(1)} fusion(f32[512,12]{0,1:T(8,128)S(1)} %bitcast.148, bf16[4608,2,12,128]{3,0,2,1:T(8,128)(2,1)} %constant_dynamic-update-slice_fusion, f32[12,4608,512]{2,1,0:T(8,128)} %get-tuple-element.20, f32[12,512]{1,0:T(8,128)S(1)} %broadcast_maximum_fusion, pred[4608]{0:T(1024)(128)(4,1)S(1)} %fusion.65), kind=kOutput, calls=%fused_computation.18 | convolution fusion | flops 7390887936 | bytes 129050624 | tf_op jit(solution)/shard_map/hqk,khd->hqd/dot_general | solution.py:78
  464.8 0.0 copy-start.11
  464.8 0.0 copy-start.12
  464.8 9.0 %fusion.74 = (f32[512]{0:T(512)S(1)}, f32[512,3072]{1,0:T(8,128)S(1)}) fusion(bf16[512,1536]{0,1:T(8,128)(2,1)S(1)} %bitcast.153, bf16[1536,3072]{1,0:T(8,128)(2,1)} %param.16, f32[3072]{0:T(1024)S(1)} %bitcast.151, bf16[512,3072]{1,0:T(8,128)(2,1)} %bitcast.152), kind=kOutput, calls=%fused_computation.111 | convolution fusion | flops 4838129152 | bytes 20461568 | tf_op jit(solution)/shard_map/dot_general | solution.py:138
  473.9 0.8 multiply_reduce_fusion
  474.7 1.4 multiply_add_fusion
  476.1 0.1 copy.70
  476.3 0.1 slice_bitcast_fusion.7
  476.4 1.3 collective-permute-start.7
  477.7 1.3 collective-permute-start.8
  479.0 0.4 fusion.40
  479.3 0.8 copy.68
  480.2 0.1 copy.72
  480.2 0.4 fusion.18
  480.6 4.7 collective-permute-done.8
  485.3 0.1 copy.73
  485.4 1.3 collective-permute-start.10
  486.7 3.0 collective-permute-start.9
  489.8 0.4 fusion.22
  490.1 0.4 collective-permute-done.9
  490.6 0.1 maximum_maximum_fusion
  490.6 0.4 fusion.33
  491.0 0.4 fusion.26
  491.3 0.4 fusion.31
  491.7 0.4 fusion.28
  492.1 0.4 fusion.15
  492.5 1.1 fusion.17
  (40 shorter events, 0.1 us)
Async XLA Ops:
  0.6 474.0 %copy-start = (bf16[3072,64]{0,1:T(8,128)(2,1)S(1)}, bf16[3072,64]{0,1:T(8,128)(2,1)}, u32[]{:S(2)}) copy-start(bf16[3072,64]{0,1:T(8,128)(2,1)} %param.17) | copy-start | bytes 1179652
  11.5 16.3 %copy-start.9 = (bf16[1,128,2,768]{3,2,1,0:T(2,128)(2,1)S(1)}, bf16[1,128,2,768]{3,2,1,0:T(2,128)(2,1)}, u32[]{:S(2)}) copy-start(bf16[1,128,2,768]{3,2,1,0:T(2,128)(2,1)} %param.12) | copy-start | bytes 1179652
  22.0 10.7 %all-to-all-start = ((bf16[16,64,3,6,128]{4,0,3,2,1:T(8,128)(2,1)}), bf16[16,64,3,6,128]{4,0,3,2,1:T(8,128)(2,1)}, u32[]{:S(2)}, u32[]{:S(2)}) async-start(bf16[16,64,3,6,128]{4,0,3,2,1:T(8,128)(2,1)} %copy.59), calls=%async_computation | async-start | bytes 9437184 | tf_op jit(solution)/shard_map/all_to_all | solution.py:127
  32.7 10.8 %all-to-all-start.1 = ((bf16[1,128,2,6,128]{4,2,3,0,1:T(2,128)(2,1)}), bf16[1,128,2,6,128]{4,2,3,0,1:T(2,128)(2,1)}, u32[]{:S(2)}, u32[]{:S(2)}) async-start(bf16[1,128,2,6,128]{4,2,3,0,1:T(2,128)(2,1)} %copy.63), calls=%async_computation.1 | async-start | bytes 786432 | tf_op jit(solution)/shard_map/all_to_all | solution.py:128
  41.0 2.1 copy-start.1
  45.3 9.5 %copy-start.8 = (bf16[1,64,2,2,6,128]{5,1,4,3,2,0:T(8,128)(2,1)S(1)}, bf16[1,64,2,2,6,128]{5,1,4,3,2,0:T(8,128)(2,1)}, u32[]{:S(2)}) copy-start(bf16[1,64,2,2,6,128]{5,1,4,3,2,0:T(8,128)(2,1)} %copy.65) | copy-start | bytes 1179652
  54.8 243.9 %copy-start.15 = (f32[29]{0:T(128)S(1)}, f32[29]{0:T(128)}, u32[]{:S(2)}) copy-start(f32[29]{0:T(128)} %param.19) | copy-start | bytes 352
  57.7 80.1 %collective-permute-start = (bf16[576,2,12,128]{3,0,2,1:T(8,128)(2,1)S(1)}, bf16[576,2,12,128]{3,0,2,1:T(8,128)(2,1)S(1)}, u32[]{:S(2)}, u32[]{:S(2)}) collective-permute-start(bf16[576,2,12,128]{3,0,2,1:T(8,128)(2,1)S(1)} %get-tuple-element.6), channel_id=1, source_target_pairs={{0,1},{1,2},{2,3},{3,4},{4,5},{5,6},{6,7},{7,0},{8,9},{9,10},{10,1... | collective-permute-start | bytes 10616840 | tf_op jit(solution)/shard_map/ppermute | solution.py:23
  58.2 81.4 %collective-permute-start.1 = (bf16[576,2,12,128]{3,0,2,1:T(8,128)(2,1)S(1)}, bf16[576,2,12,128]{3,0,2,1:T(8,128)(2,1)S(1)}, u32[]{:S(2)}, u32[]{:S(2)}) collective-permute-start(bf16[576,2,12,128]{3,0,2,1:T(8,128)(2,1)S(1)} %get-tuple-element.6), channel_id=1, source_target_pairs={{0,7},{1,0},{2,1},{3,2},{4,3},{5,4},{6,5},{7,6},{8,15},{9,8},{10,9... | collective-permute-start | bytes 10616840 | tf_op jit(solution)/shard_map/ppermute | solution.py:35
  137.9 1.8 copy-start.3
  139.6 78.3 %collective-permute-start.2 = (bf16[576,2,12,128]{3,0,2,1:T(8,128)(2,1)S(1)}, bf16[576,2,12,128]{3,0,2,1:T(8,128)(2,1)S(1)}, u32[]{:S(2)}, u32[]{:S(2)}) collective-permute-start(bf16[576,2,12,128]{3,0,2,1:T(8,128)(2,1)S(1)} %collective-permute-done), channel_id=1, source_target_pairs={{0,1},{1,2},{2,3},{3,4},{4,5},{5,6},{6,7},{7,0},{8,9},{9,10},{10,1... | collective-permute-start | bytes 10616840 | tf_op jit(solution)/shard_map/ppermute | solution.py:23
  139.6 78.3 %copy-start.4 = (bf16[576,2,12,128]{3,0,2,1:T(8,128)(2,1)}, bf16[576,2,12,128]{3,0,2,1:T(8,128)(2,1)S(1)}, u32[]{:S(2)}) copy-start(bf16[576,2,12,128]{3,0,2,1:T(8,128)(2,1)S(1)} %collective-permute-done.1) | copy-start | bytes 10616836
  139.6 78.3 %collective-permute-start.3 = (bf16[576,2,12,128]{3,0,2,1:T(8,128)(2,1)S(1)}, bf16[576,2,12,128]{3,0,2,1:T(8,128)(2,1)}, u32[]{:S(2)}, u32[]{:S(2)}) collective-permute-start(bf16[576,2,12,128]{3,0,2,1:T(8,128)(2,1)S(1)} %collective-permute-done.1), channel_id=1, source_target_pairs={{0,7},{1,0},{2,1},{3,2},{4,3},{5,4},{6,5},{7,6},{8,15},{9,8},{10,9... | collective-permute-start | bytes 10616840 | tf_op jit(solution)/shard_map/ppermute | solution.py:35
  218.0 1.8 copy-start.6
  218.0 77.7 %collective-permute-start.4 = (bf16[576,2,12,128]{3,0,2,1:T(8,128)(2,1)S(1)}, bf16[576,2,12,128]{3,0,2,1:T(8,128)(2,1)}, u32[]{:S(2)}, u32[]{:S(2)}) collective-permute-start(bf16[576,2,12,128]{3,0,2,1:T(8,128)(2,1)S(1)} %collective-permute-done.2), channel_id=1, source_target_pairs={{0,1},{1,2},{2,3},{3,4},{4,5},{5,6},{6,7},{7,0},{8,9},{9,10},{10,1... | collective-permute-start | bytes 10616840 | tf_op jit(solution)/shard_map/ppermute | solution.py:23
  219.7 101.2 %collective-permute-start.5 = (bf16[576,2,12,128]{3,0,2,1:T(8,128)(2,1)}, bf16[576,2,12,128]{3,0,2,1:T(8,128)(2,1)}, u32[]{:S(2)}, u32[]{:S(2)}) collective-permute-start(bf16[576,2,12,128]{3,0,2,1:T(8,128)(2,1)} %collective-permute-done.3), channel_id=1, source_target_pairs={{0,7},{1,0},{2,1},{3,2},{4,3},{5,4},{6,5},{7,6},{8,15},{9,8},{10,9... | collective-permute-start | bytes 10616840 | tf_op jit(solution)/shard_map/ppermute | solution.py:35
  295.7 43.0 %collective-permute-start.6 = (bf16[576,2,12,128]{3,0,2,1:T(8,128)(2,1)}, bf16[576,2,12,128]{3,0,2,1:T(8,128)(2,1)}, u32[]{:S(2)}, u32[]{:S(2)}) collective-permute-start(bf16[576,2,12,128]{3,0,2,1:T(8,128)(2,1)} %collective-permute-done.4), channel_id=1, source_target_pairs={{0,1},{1,2},{2,3},{3,4},{4,5},{5,6},{6,7},{7,0},{8,9},{9,10},{10,1... | collective-permute-start | bytes 10616840 | tf_op jit(solution)/shard_map/ppermute | solution.py:23
  298.7 8.5 %copy-start.5 = (bf16[576,2,12,128]{3,0,2,1:T(8,128)(2,1)S(1)}, bf16[576,2,12,128]{3,0,2,1:T(8,128)(2,1)}, u32[]{:S(2)}) copy-start(bf16[576,2,12,128]{3,0,2,1:T(8,128)(2,1)} %copy-done.4) | copy-start | bytes 10616836
  298.7 10.9 %copy-start.7 = (bf16[576,2,12,128]{3,0,2,1:T(8,128)(2,1)S(1)}, bf16[576,2,12,128]{3,0,2,1:T(8,128)(2,1)}, u32[]{:S(2)}) copy-start(bf16[576,2,12,128]{3,0,2,1:T(8,128)(2,1)} %copy-done.6) | copy-start | bytes 10616836
  422.2 42.6 %copy-start.14 = (f32[1,1,1,3072]{3,1,2,0:T(1,128)S(1)}, f32[1,1,1,3072]{3,1,2,0:T(1,128)}, u32[]{:S(2)}) copy-start(f32[1,1,1,3072]{3,1,2,0:T(1,128)} %get-tuple-element.9) | copy-start | bytes 36868
  464.8 9.9 %copy-start.11 = (f32[512,64]{0,1:T(8,128)S(1)}, f32[512,64]{0,1:T(8,128)}, u32[]{:S(2)}) copy-start(f32[512,64]{0,1:T(8,128)} %copy.69) | copy-start | bytes 393220
  464.8 9.9 %copy-start.12 = (f32[1,1,1,3072]{3,1,2,0:T(1,128)S(1)}, f32[1,1,1,3072]{3,1,2,0:T(1,128)}, u32[]{:S(2)}) copy-start(f32[1,1,1,3072]{3,1,2,0:T(1,128)} %get-tuple-element.8) | copy-start | bytes 36868
  464.8 9.9 %copy-start.13 = (f32[1,1,1,3072]{3,1,2,0:T(1,128)S(1)}, f32[1,1,1,3072]{3,1,2,0:T(1,128)}, u32[]{:S(2)}) copy-start(f32[1,1,1,3072]{3,1,2,0:T(1,128)} %get-tuple-element.10) | copy-start | bytes 36868
  474.7 4.3 copy-start.10
  476.3 17.3 %copy-start.2 = (f32[512,64]{1,0:T(8,128)}, f32[512,64]{1,0:T(8,128)S(1)}, u32[]{:S(2)}) copy-start(f32[512,64]{1,0:T(8,128)S(1)} %copy.70) | copy-start | bytes 393220
  476.4 3.8 collective-permute-start.7
  477.7 7.7 %collective-permute-start.8 = (f32[1,32,64]{1,2,0:T(8,128)S(1)}, f32[1,32,64]{1,2,0:T(8,128)S(1)}, u32[]{:S(2)}, u32[]{:S(2)}) collective-permute-start(f32[1,32,64]{1,2,0:T(8,128)S(1)} %get-tuple-element.16), channel_id=1, source_target_pairs={{2,0},{4,2},{6,4},{3,1},{5,3},{7,5},{10,8},{12,10},{14,12},{11,9},... | collective-permute-start | bytes 24584 | tf_op jit(solution)/shard_map/ppermute | solution.py:52
  485.4 4.7 collective-permute-start.10
  486.7 3.8 collective-permute-start.9
